TPU v7x, 256 devices: a whole 4x4x8 slice. The times are simulated.
256 devices in a mesh: ctx: 32 (over z, y_lo, core), head: 8 (over y_hi, x).
Axes of the slice: x: 4, y: 4 (y_hi: 2, y_lo: 2; y = y_hi * 2 + y_lo), z: 8, core: 2. Of those that a mesh axis runs over, the one named last changes fastest.
Arguments:
- queries: bfloat16 [512, 8192], P(('ctx', 'head')), may hold values from -150 to 150
- keys: bfloat16 [131072, 1024], P('ctx', 'head'), may hold values from -4 to 4
- values: bfloat16 [131072, 1024], P('ctx', 'head'), may hold values from -6 to 6
- doc_len: int32 [8], replicated, may hold values from 32768 to 131072, as said below
Outputs:
- attended: bfloat16 [512, 8192], P('ctx', 'head')
Inputs may be any that keep to these rules, and one draw needn't show every extreme that they name: Candidate c sees the first doc_len[c] document tokens; in every draw some candidate sees all 131072.
All inputs are finite; a program needn't handle non-finite values.
Results may differ from a plain program's by a relative error of at most 0.004.
Values may be sent and summed in bfloat16 or wider, within the bound.
No kernel may reach another device: no remote copies, remote signals or barrier semaphores. Data moves between devices by JAX's collectives and lax.ppermute only.
A program may use at most 64 MiB of HBM per device.

v0:
```python
import functools

import jax
import jax.numpy as jnp
from jax import lax
from jax.experimental import pallas as pl
from jax.experimental.pallas import tpu as pltpu
from jax.sharding import Mesh
from jax.sharding import PartitionSpec as P

HD = 128
QPK = 8
CANDS = 8
HALF = 4096
LANES = 512
CAND_LANES = 128
MEMBERS = LANES // CAND_LANES
GROUPS = CANDS // MEMBERS
SAMPLE = 128
EXTRA = 16
NONE = -1e30
LIMIT = 2.0**60
LOG2_SCALE = 1.4426950408889634 / HD**0.5
NT = (((1,), (1,)), ((), ()))
TN = (((0,), (0,)), ((), ()))


def scores(key_rows, query_rows):
    s = lax.dot_general(key_rows, query_rows, NT, preferred_element_type=jnp.float32)
    return s * LOG2_SCALE


def weighted(value_rows, weights):
    return lax.dot_general(
        value_rows, weights.astype(jnp.bfloat16), TN, preferred_element_type=jnp.float32
    )


def attend_kernel(
    info, q_ref, k_own, k_other, v_own, v_other, out_ref, top_ref, acc_ref, sum_ref, big_ref
):
    base_own, base_other, part = info[CANDS], info[CANDS + 1], info[CANDS + 2]
    base = jnp.minimum(base_own, base_other)
    end = base + 2 * HALF
    halves = ((k_own, v_own, base_own), (k_other, v_other, base_other))
    lane = lax.broadcasted_iota(jnp.int32, (1, LANES), 1)

    def visible(group):
        seen = info[group * MEMBERS]
        for j in range(1, MEMBERS):
            seen = jnp.where(lane < j * CAND_LANES, seen, info[group * MEMBERS + j])
        return seen

    def group_queries(group):
        rows = [q_ref[group * MEMBERS + j, part] for j in range(MEMBERS)]
        return jnp.concatenate(rows, axis=0)

    def store(group, numerators, total, top):
        extra = split_total(total, top, LANES)
        for j in range(MEMBERS):
            cut = slice(j * HD, (j + 1) * HD)
            out_ref[group * MEMBERS + j, :HD, :] = numerators[:, cut].astype(jnp.bfloat16)
            out_ref[group * MEMBERS + j, HD:, :] = extra[:, cut]

    first_keys = jnp.where(base_own == base, k_own[:SAMPLE, :], k_other[:SAMPLE, :])
    place = base + lax.broadcasted_iota(jnp.int32, (SAMPLE, LANES), 0)
    for group in range(GROUPS):
        s = scores(first_keys, group_queries(group))
        top = jnp.max(jnp.where(place < visible(group), s, NONE), axis=0, keepdims=True)
        top_ref[group] = top.astype(jnp.bfloat16).astype(jnp.float32)
    big_ref[...] = jnp.zeros_like(big_ref)

    def one_pass(group, masked):
        query_rows = group_queries(group)
        top = top_ref[group]
        point = jnp.where(top > 0.5 * NONE, top, -NONE)
        seen = visible(group)
        total = jnp.zeros((8, LANES), jnp.float32)
        numerators = jnp.zeros((HD, LANES), jnp.float32)
        for k_ref, v_ref, start in halves:
            weights = jnp.exp2(scores(k_ref[...], query_rows) - point)
            if masked:
                place = start + lax.broadcasted_iota(jnp.int32, (HALF, LANES), 0)
                weights = jnp.where(place < seen, weights, 0.0)
            total += jnp.sum(weights.reshape(HALF // 8, 8, LANES), axis=0)
            numerators += weighted(v_ref[...], weights)
        total = jnp.sum(total, axis=0, keepdims=True)
        big_ref[...] = jnp.maximum(big_ref[...], total)
        store(group, numerators, total, top)

    @pl.loop(0, GROUPS)
    def _(group):
        lengths = [info[group * MEMBERS + j] for j in range(MEMBERS)]
        idle = functools.reduce(jnp.maximum, lengths) <= base
        whole = functools.reduce(
            jnp.logical_and, [jnp.logical_or(n <= base, n >= end) for n in lengths]
        )
        plain = jnp.logical_and(whole, jnp.logical_not(idle))
        mixed = jnp.logical_not(whole)

        @pl.when(idle)
        def _():
            nothing = jnp.zeros((1, LANES), jnp.float32)
            store(group, jnp.zeros((HD, LANES), jnp.float32), nothing, nothing + NONE)

        @pl.when(plain)
        def _():
            one_pass(group, False)

        @pl.when(mixed)
        def _():
            one_pass(group, True)

    @pl.when(jnp.logical_not(jnp.max(big_ref[...]) < LIMIT))
    def _():
        block = 512

        @pl.loop(0, GROUPS)
        def _(group):
            query_rows = group_queries(group)
            seen = visible(group)
            acc_ref[...] = jnp.zeros_like(acc_ref)
            sum_ref[...] = jnp.zeros_like(sum_ref)
            top_ref[group] = jnp.full((1, LANES), NONE, jnp.float32)
            for k_ref, v_ref, start in halves:

                @pl.loop(0, HALF // block)
                def _(i):
                    at = pl.multiple_of(i * block, block)
                    place = start + at + lax.broadcasted_iota(jnp.int32, (block, LANES), 0)
                    usable = place < seen
                    s = jnp.where(usable, scores(k_ref[pl.ds(at, block), :], query_rows), NONE)
                    old = top_ref[group]
                    new = jnp.maximum(old, jnp.max(s, axis=0, keepdims=True))
                    shrink = jnp.exp2(old - new)
                    weights = jnp.where(usable, jnp.exp2(s - new), 0.0)
                    sum_ref[...] = sum_ref[...] * shrink + jnp.sum(
                        weights.reshape(block // 8, 8, LANES), axis=0
                    )
                    acc_ref[...] = acc_ref[...] * shrink + weighted(
                        v_ref[pl.ds(at, block), :], weights
                    )
                    top_ref[group] = new

            top = top_ref[group]
            sent = top.astype(jnp.bfloat16).astype(jnp.float32)
            fit = jnp.where(top > 0.5 * NONE, jnp.exp2(top - sent), 1.0)
            total = jnp.sum(sum_ref[...], axis=0, keepdims=True)
            store(group, acc_ref[...] * fit, total * fit, sent)


def split_total(total, top, width):
    total_high = total.astype(jnp.bfloat16).astype(jnp.float32)
    row = lax.broadcasted_iota(jnp.int32, (EXTRA, width), 0)
    extra = jnp.where(row == 0, top, 0.0)
    extra = jnp.where(row == 1, total_high, extra)
    return jnp.where(row == 2, total - total_high, extra).astype(jnp.bfloat16)


def summed(pieces):
    extras = [piece[HD:, :].astype(jnp.float32) for piece in pieces]
    top = functools.reduce(jnp.maximum, [extra[0:1] for extra in extras])
    total = jnp.zeros((1, HD), jnp.float32)
    numerators = jnp.zeros((HD, HD), jnp.float32)
    for piece, extra in zip(pieces, extras, strict=True):
        scale = jnp.exp2(extra[0:1] - top)
        total += scale * (extra[1:2] + extra[2:3])
        numerators += scale * piece[:HD, :].astype(jnp.float32)
    return numerators, total, top


def merge_kernel(a_ref, b_ref, out_ref):
    for i in range(out_ref.shape[0]):
        numerators, total, top = summed([a_ref[i], b_ref[i]])
        out_ref[i, :HD, :] = numerators.astype(jnp.bfloat16)
        out_ref[i, HD:, :] = split_total(total, top, HD)


def combine_kernel(x_ref, out_ref, turned_ref):
    numerators, total, _ = summed([x_ref[i] for i in range(x_ref.shape[0])])
    turned_ref[...] = (numerators / total).T
    for h in range(QPK):
        rows = turned_ref[pl.ds(h, HD // QPK, stride=QPK), :]
        out_ref[:, h * HD : (h + 1) * HD] = rows.astype(jnp.bfloat16)


def attend(info, q, k_own, k_other, v_own, v_other):
    in_vmem = pl.BlockSpec(memory_space=pltpu.VMEM)
    work = q.size // HD // 2 * 2 * HALF
    return pl.pallas_call(
        attend_kernel,
        out_shape=jax.ShapeDtypeStruct((CANDS, HD + EXTRA, HD), jnp.bfloat16),
        in_specs=[pl.BlockSpec(memory_space=pltpu.SMEM)] + [in_vmem] * 5,
        out_specs=in_vmem,
        scratch_shapes=[
            pltpu.VMEM((GROUPS, 1, LANES), jnp.float32),
            pltpu.VMEM((HD, LANES), jnp.float32),
            pltpu.VMEM((8, LANES), jnp.float32),
            pltpu.VMEM((1, LANES), jnp.float32),
        ],
        compiler_params=pltpu.CompilerParams(vmem_limit_bytes=32 * 2**20),
        cost_estimate=pl.CostEstimate(
            flops=4 * work * HD, bytes_accessed=6 * 2**20, transcendentals=work
        ),
        name="attend",
    )(info, q, k_own, k_other, v_own, v_other)


def merge(a, b):
    in_vmem = pl.BlockSpec(memory_space=pltpu.VMEM)
    return pl.pallas_call(
        merge_kernel,
        out_shape=jax.ShapeDtypeStruct(a.shape, jnp.bfloat16),
        in_specs=[in_vmem] * 2,
        out_specs=in_vmem,
        compiler_params=pltpu.CompilerParams(vmem_limit_bytes=8 * 2**20),
        cost_estimate=pl.CostEstimate(
            flops=8 * a.size, bytes_accessed=6 * a.size, transcendentals=0
        ),
        name="merge",
    )(a, b)


def combine(x):
    in_vmem = pl.BlockSpec(memory_space=pltpu.VMEM)
    return pl.pallas_call(
        combine_kernel,
        out_shape=jax.ShapeDtypeStruct((HD // QPK, QPK * HD), jnp.bfloat16),
        in_specs=[in_vmem],
        out_specs=in_vmem,
        scratch_shapes=[pltpu.VMEM((HD, HD), jnp.float32)],
        compiler_params=pltpu.CompilerParams(vmem_limit_bytes=8 * 2**20),
        cost_estimate=pl.CostEstimate(
            flops=4 * x.size, bytes_accessed=2 * x.size, transcendentals=0
        ),
        name="combine",
    )(x)


def body(queries, keys, values, doc_len):
    swap = [(0, 1), (1, 0)]
    k_other = lax.ppermute(keys, "c", swap)
    v_other = lax.ppermute(values, "c", swap)

    rows = queries.shape[0]
    heads = lax.axis_size(("h", "x"))
    spans = lax.axis_size(("z", "y"))
    blocks = queries.reshape(rows, heads, QPK, HD).transpose(1, 0, 2, 3)
    blocks = blocks.reshape(1, heads, rows * QPK, HD)
    blocks = jnp.broadcast_to(blocks, (spans, heads, rows * QPK, HD))
    q = lax.all_to_all(
        blocks.reshape(spans * heads, rows * QPK, HD), ("z", "y", "h", "x"), 0, 0
    ).reshape(CANDS, spans // CANDS, heads * rows * QPK, HD)

    chip = lax.axis_index(("z", "y")) * (2 * HALF)
    core, side = lax.axis_index("c"), lax.axis_index("y")
    bases = [chip + core * HALF, chip + (1 - core) * HALF]

    def info(part):
        return jnp.concatenate([doc_len, jnp.stack(bases + [part]).astype(jnp.int32)])

    foreign = attend(info(1 - side), q, keys, k_other, values, v_other)
    received = lax.ppermute(foreign, "y", swap)
    own = attend(info(side), q, keys, k_other, values, v_other)
    return combine(lax.all_to_all(merge(own, received), "z", 0, 0))


def solution(mesh):
    fine = Mesh(mesh.devices.reshape(8, 2, 2, 2, 4), ("z", "y", "c", "h", "x"))
    ctx, head = ("z", "y", "c"), ("h", "x")
    placed = (P(ctx + head, None), P(ctx, head), P(ctx, head), P())
    return jax.shard_map(
        body, mesh=fine, in_specs=placed, out_specs=P(ctx, head), check_vma=False
    )
```

profile of v0, /device:TPU:2, one launch (start us, length us, event | category | flops | bytes accessed | tf_op | source)
XLA Modules:
  0.0 125.6 jit_solution(13303695338900730214)
XLA Ops:
  0.0 0.0 copy-start
  0.0 0.0 collective-permute-start
  0.0 0.5 collective-permute-start.1
  0.5 0.8 copy_bitcast_fusion
  1.3 0.9 broadcast_in_dim.8
  2.2 15.4 %all-to-all-start = ((bf16[128,16,128]{2,1,0:T(8,128)(2,1)}), bf16[128,16,128]{2,1,0:T(8,128)(2,1)S(1)}, u32[]{:S(2)}, u32[]{:S(2)}) async-start(bf16[128,16,128]{2,1,0:T(8,128)(2,1)} %bitcast.5), calls=%async_computation | async-start | bytes 1048576 | tf_op jit(solution)/shard_map/all_to_all | solution.py:251
  17.7 0.0 copy-start.3
  17.7 0.6 copy-done.3
  18.3 0.1 pad_add_fusion.2
  18.4 0.1 pad_add_fusion.info
  18.5 18.0 %all-to-all-done = bf16[128,16,128]{2,1,0:T(8,128)(2,1)S(1)} async-done(((bf16[128,16,128]{2,1,0:T(8,128)(2,1)}), bf16[128,16,128]{2,1,0:T(8,128)(2,1)S(1)}, u32[]{:S(2)}, u32[]{:S(2)}) %all-to-all-start) | async-done | bytes 524320 | tf_op jit(solution)/shard_map/all_to_all | solution.py:251
  36.5 0.0 collective-permute-done.k_other
  36.5 0.0 collective-permute-done.1.v_other
  36.5 0.0 copy-done
  36.5 0.0 copy-start.1
  36.5 1.2 copy-done.1
  37.7 0.0 copy-start.2
  37.7 34.6 %attend.3 = bf16[8,144,128]{2,1,0:T(8,128)(2,1)S(1)} custom-call(s32[11]{0:T(128)S(1)} %get-tuple-element.5.info, bf16[8,2,128,128]{3,2,1,0:T(8,128)(2,1)S(1)} %bitcast.16, bf16[4096,128]{1,0:T(8,128)(2,1)S(1)} %copy-done, bf16[4096,128]{1,0:T(8,128)(2,1)S(1)} %collective-permute-done.k_other, bf16[4096,128]{1,0:T(8,128)(2,1)S(1)} %copy-done.1, ...), custom_call_target="tpu_custom_call" | custom-call | flops 4294967296 | bytes 6291456 | tf_op jit(solution)/shard_map/attend/pallas_call | solution.py:190
  72.3 1.0 collective-permute-start.2
  73.4 0.0 copy-done.2
  73.4 34.6 %attend.2.a_ref = bf16[8,144,128]{2,1,0:T(8,128)(2,1)S(1)} custom-call(s32[11]{0:T(128)S(1)} %pad_add_fusion.info, bf16[8,2,128,128]{3,2,1,0:T(8,128)(2,1)S(1)} %bitcast.17, bf16[4096,128]{1,0:T(8,128)(2,1)S(1)} %copy-done, bf16[4096,128]{1,0:T(8,128)(2,1)S(1)} %collective-permute-done.k_other, bf16[4096,128]{1,0:T(8,128)(2,1)S(1)} %copy-done.2, ...), custom_call_target="tpu_custom_call" | custom-call | flops 4294967296 | bytes 6291456 | tf_op jit(solution)/shard_map/attend/pallas_call | solution.py:190
  108.0 0.0 collective-permute-done.2.b_ref
  108.0 0.1 merge.1
  108.1 16.7 %all_to_all.10.x_ref = bf16[8,144,128]{2,1,0:T(8,128)(2,1)S(1)} all-to-all(bf16[8,144,128]{2,1,0:T(8,128)(2,1)S(1)} %merge.1), channel_id=1, replica_groups=mesh['z'=8,'y'=2,'c'=2,'h'=2,'x'=4] {'z'}, dimensions={0} | all-to-all | bytes 589824 | tf_op jit(solution)/shard_map/all_to_all | solution.py:265
  124.9 0.8 combine.1
Async XLA Ops:
  0.0 36.5 %copy-start = (bf16[4096,128]{1,0:T(8,128)(2,1)S(1)}, bf16[4096,128]{1,0:T(8,128)(2,1)}, u32[]{:S(2)}) copy-start(bf16[4096,128]{1,0:T(8,128)(2,1)} %k_own.3) | copy-start | bytes 3145732
  0.0 36.5 %collective-permute-start = (bf16[4096,128]{1,0:T(8,128)(2,1)}, bf16[4096,128]{1,0:T(8,128)(2,1)S(1)}, u32[]{:S(2)}, u32[]{:S(2)}) collective-permute-start(bf16[4096,128]{1,0:T(8,128)(2,1)} %k_own.3), channel_id=1, source_target_pairs={{0,8},{8,0},{1,9},{9,1},{2,10},{10,2},{3,11},{11,3},{4,12},{12,4},... | collective-permute-start | bytes 3145736 | tf_op jit(solution)/shard_map/ppermute | solution.py:242
  0.0 36.5 %collective-permute-start.1 = (bf16[4096,128]{1,0:T(8,128)(2,1)}, bf16[4096,128]{1,0:T(8,128)(2,1)}, u32[]{:S(2)}, u32[]{:S(2)}) collective-permute-start(bf16[4096,128]{1,0:T(8,128)(2,1)} %v_own.3), channel_id=1, source_target_pairs={{0,8},{8,0},{1,9},{9,1},{2,10},{10,2},{3,11},{11,3},{4,12},{12,4},... | collective-permute-start | bytes 3145736 | tf_op jit(solution)/shard_map/ppermute | solution.py:243
  2.2 34.3 %all-to-all-start = ((bf16[128,16,128]{2,1,0:T(8,128)(2,1)}), bf16[128,16,128]{2,1,0:T(8,128)(2,1)S(1)}, u32[]{:S(2)}, u32[]{:S(2)}) async-start(bf16[128,16,128]{2,1,0:T(8,128)(2,1)} %bitcast.5), calls=%async_computation | async-start | bytes 1048576 | tf_op jit(solution)/shard_map/all_to_all | solution.py:251
  17.7 0.7 copy-start.3
  36.5 1.2 copy-start.1
  37.7 35.6 %copy-start.2 = (bf16[4096,128]{1,0:T(8,128)(2,1)S(1)}, bf16[4096,128]{1,0:T(8,128)(2,1)}, u32[]{:S(2)}) copy-start(bf16[4096,128]{1,0:T(8,128)(2,1)} %v_own.3) | copy-start | bytes 3145732
  72.3 35.6 %collective-permute-start.2 = (bf16[8,144,128]{2,1,0:T(8,128)(2,1)S(1)}, bf16[8,144,128]{2,1,0:T(8,128)(2,1)S(1)}, u32[]{:S(2)}, u32[]{:S(2)}) collective-permute-start(bf16[8,144,128]{2,1,0:T(8,128)(2,1)S(1)} %attend.3), channel_id=1, source_target_pairs={{0,16},{16,0},{1,17},{17,1},{2,18},{18,2},{3,19},{19,3},{4,20},{20... | collective-permute-start | bytes 884744 | tf_op jit(solution)/shard_map/ppermute | solution.py:263
where the time goes:
time: 128 us; the launch traced here: 126 us
  Pallas kernels  70.1 us (55%)
  waiting for transfers between devices  18 us (14%)
  starting transfers between devices  17 us (13%)
  blocking collectives  16.7 us (13%)
  local copies, waits for them, and re-layouts  3.56 us (3%)
    pallas_call x2, Pallas kernels, attend(): pl.pallas_call(attend_kernel, out_shape=jax.ShapeDtypeStruct((CANDS, HD +...  69.2 us
    all_to_all x1, waiting for transfers between devices, body(): lax.all_to_all(blocks.reshape(spans * heads, rows * QPK, HD), ('z', 'y',...  18 us
    all_to_all x1, blocking collectives, body(): return combine(lax.all_to_all(merge(own, received), 'z', 0, 0))  16.7 us
    all_to_all x1, starting transfers between devices, body(): lax.all_to_all(blocks.reshape(spans * heads, rows * QPK, HD), ('z', 'y',...  15.4 us
  transfers between devices with their start and end apart: 4, of which 1 were waited for; matrix products, arithmetic and copies ran while one was open for 1% of the time, Pallas kernels for 28%

commit v1 on v0

--- a/solution.py
+++ b/solution.py
@@ -12,13 +12,14 @@
 QPK = 8
 CANDS = 8
 HALF = 4096
-LANES = 512
+LANES = 1024
 CAND_LANES = 128
 MEMBERS = LANES // CAND_LANES
 GROUPS = CANDS // MEMBERS
 SAMPLE = 128
 EXTRA = 16
 NONE = -1e30
+HIDDEN = -(2.0**100)
 LIMIT = 2.0**60
 LOG2_SCALE = 1.4426950408889634 / HD**0.5
 NT = (((1,), (1,)), ((), ()))
@@ -36,13 +37,24 @@
     )
 
 
-def attend_kernel(
-    info, q_ref, k_own, k_other, v_own, v_other, out_ref, top_ref, acc_ref, sum_ref, big_ref
-):
+def block_kernel(q_ref, out_ref, rows_ref):
+    rows, heads = q_ref.shape[0], q_ref.shape[1] // (QPK * HD)
+    q = q_ref[...].astype(jnp.float32)
+    for g in range(heads):
+        for i in range(rows):
+            for h in range(QPK):
+                at = (g * rows + i) * QPK + h
+                cut = slice((g * QPK + h) * HD, (g * QPK + h + 1) * HD)
+                rows_ref[at : at + 1, :] = q[i : i + 1, cut]
+    blocks = rows_ref[...].astype(jnp.bfloat16).reshape(heads, rows * QPK, HD)
+    for j in range(out_ref.shape[0]):
+        out_ref[j] = blocks
+
+
+def attend_kernel(info, q_ref, k_ref, v_ref, out_ref, top_ref, acc_ref, sum_ref, big_ref):
     base_own, base_other, part = info[CANDS], info[CANDS + 1], info[CANDS + 2]
     base = jnp.minimum(base_own, base_other)
-    end = base + 2 * HALF
-    halves = ((k_own, v_own, base_own), (k_other, v_other, base_other))
+    halves = ((0, base_own), (HALF, base_other))
     lane = lax.broadcasted_iota(jnp.int32, (1, LANES), 1)
 
     def visible(group):
@@ -59,10 +71,11 @@
         extra = split_total(total, top, LANES)
         for j in range(MEMBERS):
             cut = slice(j * HD, (j + 1) * HD)
-            out_ref[group * MEMBERS + j, :HD, :] = numerators[:, cut].astype(jnp.bfloat16)
-            out_ref[group * MEMBERS + j, HD:, :] = extra[:, cut]
-
-    first_keys = jnp.where(base_own == base, k_own[:SAMPLE, :], k_other[:SAMPLE, :])
+            out_ref[group * MEMBERS + j, :HD, :] = numerators[:, cut].astype(out_ref.dtype)
+            out_ref[group * MEMBERS + j, HD:, :] = extra[:, cut].astype(out_ref.dtype)
+
+    first = pl.multiple_of(jnp.where(base_own == base, 0, HALF), HALF)
+    first_keys = k_ref[pl.ds(first, SAMPLE), :]
     place = base + lax.broadcasted_iota(jnp.int32, (SAMPLE, LANES), 0)
     for group in range(GROUPS):
         s = scores(first_keys, group_queries(group))
@@ -70,46 +83,42 @@
         top_ref[group] = top.astype(jnp.bfloat16).astype(jnp.float32)
     big_ref[...] = jnp.zeros_like(big_ref)
 
-    def one_pass(group, masked):
-        query_rows = group_queries(group)
-        top = top_ref[group]
-        point = jnp.where(top > 0.5 * NONE, top, -NONE)
-        seen = visible(group)
-        total = jnp.zeros((8, LANES), jnp.float32)
-        numerators = jnp.zeros((HD, LANES), jnp.float32)
-        for k_ref, v_ref, start in halves:
-            weights = jnp.exp2(scores(k_ref[...], query_rows) - point)
-            if masked:
-                place = start + lax.broadcasted_iota(jnp.int32, (HALF, LANES), 0)
-                weights = jnp.where(place < seen, weights, 0.0)
-            total += jnp.sum(weights.reshape(HALF // 8, 8, LANES), axis=0)
-            numerators += weighted(v_ref[...], weights)
-        total = jnp.sum(total, axis=0, keepdims=True)
-        big_ref[...] = jnp.maximum(big_ref[...], total)
-        store(group, numerators, total, top)
-
     @pl.loop(0, GROUPS)
     def _(group):
         lengths = [info[group * MEMBERS + j] for j in range(MEMBERS)]
         idle = functools.reduce(jnp.maximum, lengths) <= base
-        whole = functools.reduce(
-            jnp.logical_and, [jnp.logical_or(n <= base, n >= end) for n in lengths]
-        )
-        plain = jnp.logical_and(whole, jnp.logical_not(idle))
-        mixed = jnp.logical_not(whole)
 
         @pl.when(idle)
         def _():
             nothing = jnp.zeros((1, LANES), jnp.float32)
             store(group, jnp.zeros((HD, LANES), jnp.float32), nothing, nothing + NONE)
 
-        @pl.when(plain)
+        @pl.when(jnp.logical_not(idle))
         def _():
-            one_pass(group, False)
-
-        @pl.when(mixed)
-        def _():
-            one_pass(group, True)
+            column = lax.broadcasted_iota(jnp.int32, (1, HD), 1)
+            limit = functools.reduce(
+                lambda rest, j: jnp.where(column == j, lengths[j], rest),
+                range(MEMBERS),
+                jnp.full((1, HD), 2**30, jnp.int32),
+            )
+            member = lax.broadcasted_iota(jnp.int32, (LANES, HD), 0) // CAND_LANES
+            column = lax.broadcasted_iota(jnp.int32, (LANES, HD), 1)
+            veto = jnp.where(member == column, HIDDEN, 0.0).astype(jnp.bfloat16)
+            query_rows = jnp.concatenate([group_queries(group), veto], axis=1)
+            top = top_ref[group]
+            point = jnp.where(top > 0.5 * NONE, top, -NONE)
+            total = jnp.zeros((8, LANES), jnp.float32)
+            numerators = jnp.zeros((HD, LANES), jnp.float32)
+            for half, start in halves:
+                place = start + lax.broadcasted_iota(jnp.int32, (HALF, HD), 0)
+                unseen = jnp.where(place >= limit, 1.0, 0.0).astype(jnp.bfloat16)
+                key_rows = jnp.concatenate([k_ref[half : half + HALF, :], unseen], axis=1)
+                weights = jnp.exp2(scores(key_rows, query_rows) - point)
+                total += jnp.sum(weights.reshape(HALF // 8, 8, LANES), axis=0)
+                numerators += weighted(v_ref[half : half + HALF, :], weights)
+            total = jnp.sum(total, axis=0, keepdims=True)
+            big_ref[...] = jnp.maximum(big_ref[...], total)
+            store(group, numerators, total, top)
 
     @pl.when(jnp.logical_not(jnp.max(big_ref[...]) < LIMIT))
     def _():
@@ -122,12 +131,12 @@
             acc_ref[...] = jnp.zeros_like(acc_ref)
             sum_ref[...] = jnp.zeros_like(sum_ref)
             top_ref[group] = jnp.full((1, LANES), NONE, jnp.float32)
-            for k_ref, v_ref, start in halves:
+            for half, start in halves:
 
                 @pl.loop(0, HALF // block)
                 def _(i):
-                    at = pl.multiple_of(i * block, block)
-                    place = start + at + lax.broadcasted_iota(jnp.int32, (block, LANES), 0)
+                    at = pl.multiple_of(half + i * block, block)
+                    place = start + i * block + lax.broadcasted_iota(jnp.int32, (block, LANES), 0)
                     usable = place < seen
                     s = jnp.where(usable, scores(k_ref[pl.ds(at, block), :], query_rows), NONE)
                     old = top_ref[group]
@@ -184,13 +193,30 @@
         out_ref[:, h * HD : (h + 1) * HD] = rows.astype(jnp.bfloat16)
 
 
-def attend(info, q, k_own, k_other, v_own, v_other):
+def build_blocks(queries, heads, spans):
+    in_vmem = pl.BlockSpec(memory_space=pltpu.VMEM)
+    rows = queries.shape[0] * QPK
+    return pl.pallas_call(
+        block_kernel,
+        out_shape=jax.ShapeDtypeStruct((spans, heads, rows, HD), jnp.bfloat16),
+        in_specs=[in_vmem],
+        out_specs=in_vmem,
+        scratch_shapes=[pltpu.VMEM((heads * rows, HD), jnp.float32)],
+        compiler_params=pltpu.CompilerParams(vmem_limit_bytes=8 * 2**20),
+        cost_estimate=pl.CostEstimate(
+            flops=0, bytes_accessed=2 * spans * queries.size, transcendentals=0
+        ),
+        name="build_blocks",
+    )(queries)
+
+
+def attend(info, q, k, v, dtype):
     in_vmem = pl.BlockSpec(memory_space=pltpu.VMEM)
     work = q.size // HD // 2 * 2 * HALF
     return pl.pallas_call(
         attend_kernel,
-        out_shape=jax.ShapeDtypeStruct((CANDS, HD + EXTRA, HD), jnp.bfloat16),
-        in_specs=[pl.BlockSpec(memory_space=pltpu.SMEM)] + [in_vmem] * 5,
+        out_shape=jax.ShapeDtypeStruct((CANDS, HD + EXTRA, HD), dtype),
+        in_specs=[pl.BlockSpec(memory_space=pltpu.SMEM)] + [in_vmem] * 3,
         out_specs=in_vmem,
         scratch_shapes=[
             pltpu.VMEM((GROUPS, 1, LANES), jnp.float32),
@@ -198,12 +224,12 @@
             pltpu.VMEM((8, LANES), jnp.float32),
             pltpu.VMEM((1, LANES), jnp.float32),
         ],
-        compiler_params=pltpu.CompilerParams(vmem_limit_bytes=32 * 2**20),
+        compiler_params=pltpu.CompilerParams(vmem_limit_bytes=40 * 2**20),
         cost_estimate=pl.CostEstimate(
             flops=4 * work * HD, bytes_accessed=6 * 2**20, transcendentals=work
         ),
         name="attend",
-    )(info, q, k_own, k_other, v_own, v_other)
+    )(info, q, k, v)
 
 
 def merge(a, b):
@@ -239,18 +265,15 @@
 
 def body(queries, keys, values, doc_len):
     swap = [(0, 1), (1, 0)]
-    k_other = lax.ppermute(keys, "c", swap)
-    v_other = lax.ppermute(values, "c", swap)
-
-    rows = queries.shape[0]
+    k = jnp.concatenate([keys, lax.ppermute(keys, "c", swap)], axis=0)
+    v = jnp.concatenate([values, lax.ppermute(values, "c", swap)], axis=0)
+
     heads = lax.axis_size(("h", "x"))
     spans = lax.axis_size(("z", "y"))
-    blocks = queries.reshape(rows, heads, QPK, HD).transpose(1, 0, 2, 3)
-    blocks = blocks.reshape(1, heads, rows * QPK, HD)
-    blocks = jnp.broadcast_to(blocks, (spans, heads, rows * QPK, HD))
+    blocks = build_blocks(queries, heads, spans)
     q = lax.all_to_all(
-        blocks.reshape(spans * heads, rows * QPK, HD), ("z", "y", "h", "x"), 0, 0
-    ).reshape(CANDS, spans // CANDS, heads * rows * QPK, HD)
+        blocks.reshape((spans * heads,) + blocks.shape[2:]), ("z", "y", "h", "x"), 0, 0
+    ).reshape(CANDS, spans // CANDS, CAND_LANES, HD)
 
     chip = lax.axis_index(("z", "y")) * (2 * HALF)
     core, side = lax.axis_index("c"), lax.axis_index("y")
@@ -259,9 +282,9 @@
     def info(part):
         return jnp.concatenate([doc_len, jnp.stack(bases + [part]).astype(jnp.int32)])
 
-    foreign = attend(info(1 - side), q, keys, k_other, values, v_other)
+    foreign = attend(info(1 - side), q, k, v, jnp.bfloat16)
     received = lax.ppermute(foreign, "y", swap)
-    own = attend(info(side), q, keys, k_other, values, v_other)
+    own = attend(info(side), q, k, v, jnp.float32)
     return combine(lax.all_to_all(merge(own, received), "z", 0, 0))
 
 

time: 128 us -> 115 us (0.90)
  Pallas kernels: 70.1 us -> 61.4 us
  waiting for transfers between devices: 18 us -> 13.3 us
  local copies, waits for them, and re-layouts: 3.56 us -> 6.88 us
  blocking collectives: 16.7 us -> 13.7 us
    pallas_call x2, Pallas kernels: 69.2 us -> 59.6 us  [attend(): pl.pallas_call(attend_kernel, out_shape=jax.ShapeDtypeStruct((CANDS, HD +...]
    all_to_all x1, waiting for transfers between devices: 18 us -> 13.3 us  [body(): lax.all_to_all(blocks.reshape((spans * heads,) + blocks.shape[2:]), ('z',...]
    all_to_all x1, blocking collectives: 16.7 us -> 13.7 us  [body(): return combine(lax.all_to_all(merge(own, received), 'z', 0, 0))]
    concatenate x0 -> x2, local copies, waits for them, and re-layouts: none -> 2.72 us  [the longest x1 1.36 us: body(): k = jnp.concatenate([keys, lax.ppermute(keys, 'c', swap)], axis=0)]
    unnamed x8 -> x14, local copies, waits for them, and re-layouts: 1.88 us -> 4.15 us
    broadcast_in_dim x2 -> x0, local copies, waits for them, and re-layouts: 1.69 us -> none  [body(): blocks = jnp.broadcast_to(blocks, (spans, heads, rows * QPK, HD))]
  transfers between devices with their start and end apart: 4 -> 4, of which waited for: 1 -> 1; matrix products, arithmetic and copies ran while one was open for 1% -> 3% of each run, Pallas kernels for 28% -> 27%
where the time goes in v1:
time: 115 us; the launch traced here: 113 us
  Pallas kernels  61.4 us (53%)
  starting transfers between devices  16.9 us (15%)
  blocking collectives  13.7 us (12%)
  waiting for transfers between devices  13.3 us (12%)
  local copies, waits for them, and re-layouts  6.88 us (6%)
    pallas_call x2, Pallas kernels, attend(): pl.pallas_call(attend_kernel, out_shape=jax.ShapeDtypeStruct((CANDS, HD +...  59.6 us
    all_to_all x1, starting transfers between devices, body(): lax.all_to_all(blocks.reshape((spans * heads,) + blocks.shape[2:]), ('z',...  15.4 us
    all_to_all x1, blocking collectives, body(): return combine(lax.all_to_all(merge(own, received), 'z', 0, 0))  13.7 us
    all_to_all x1, waiting for transfers between devices, body(): lax.all_to_all(blocks.reshape((spans * heads,) + blocks.shape[2:]), ('z',...  13.3 us
    unnamed x14, local copies, waits for them, and re-layouts  4.15 us
  transfers between devices with their start and end apart: 4, of which 1 were waited for; matrix products, arithmetic and copies ran while one was open for 3% of the time, Pallas kernels for 27%

profile of v1, /device:TPU:2, one launch (start us, length us, event | category | flops | bytes accessed | tf_op | source)
XLA Modules:
  0.0 113.2 jit_solution(14655328903708740917)
XLA Ops:
  0.0 0.0 collective-permute-start
  0.0 0.5 collective-permute-start.1
  0.5 0.0 copy-start.3
  0.5 0.8 copy-done.3
  1.3 0.0 copy-start.4
  1.3 0.9 build_blocks.1
  2.2 15.4 %all-to-all-start = ((bf16[128,16,128]{2,1,0:T(8,128)(2,1)}), bf16[128,16,128]{2,1,0:T(8,128)(2,1)S(1)}, u32[]{:S(2)}, u32[]{:S(2)}) async-start(bf16[128,16,128]{2,1,0:T(8,128)(2,1)} %bitcast.3), calls=%async_computation | async-start | bytes 1048576 | tf_op jit(solution)/shard_map/all_to_all | solution.py:274
  17.6 0.0 copy-start.5
  17.6 0.8 pad_add_fusion.2
  18.5 0.0 copy-done.4
  18.5 0.1 constant_dynamic-update-slice_fusion.1
  18.5 0.3 copy-done.5
  18.9 0.1 constant_dynamic-update-slice_fusion.3
  18.9 0.1 pad_add_fusion.info
  19.0 0.0 collective-permute-done
  19.0 1.4 %constant_dynamic-update-slice_fusion.k_ref = bf16[8192,128]{1,0:T(8,128)(2,1)S(1)} fusion(bf16[8192,128]{1,0:T(8,128)(2,1)S(1)} %constant_dynamic-update-slice_fusion.1, bf16[4096,128]{1,0:T(8,128)(2,1)} %collective-permute-done), kind=kLoop, calls=%fused_computation | loop fusion | bytes 2097152 | tf_op jit(solution)/shard_map/concatenate | solution.py:268
  20.4 0.0 copy-start
  20.4 1.3 %copy-done = bf16[8192,128]{1,0:T(8,128)(2,1)} copy-done((bf16[8192,128]{1,0:T(8,128)(2,1)}, bf16[8192,128]{1,0:T(8,128)(2,1)S(1)}, u32[]{:S(2)}) %copy-start) | copy-done | bytes 2097176
  21.7 0.0 collective-permute-done.1
  21.7 1.4 %constant_dynamic-update-slice_fusion.2.v_ref = bf16[8192,128]{1,0:T(8,128)(2,1)S(1)} fusion(bf16[8192,128]{1,0:T(8,128)(2,1)S(1)} %constant_dynamic-update-slice_fusion.3, bf16[4096,128]{1,0:T(8,128)(2,1)} %collective-permute-done.1), kind=kLoop, calls=%fused_computation.2 | loop fusion | bytes 2097152 | tf_op jit(solution)/shard_map/concatenate | solution.py:269
  23.1 13.3 %all-to-all-done = bf16[128,16,128]{2,1,0:T(8,128)(2,1)S(1)} async-done(((bf16[128,16,128]{2,1,0:T(8,128)(2,1)}), bf16[128,16,128]{2,1,0:T(8,128)(2,1)S(1)}, u32[]{:S(2)}, u32[]{:S(2)}) %all-to-all-start) | async-done | bytes 524320 | tf_op jit(solution)/shard_map/all_to_all | solution.py:274
  36.4 0.0 copy-start.1
  36.4 1.6 %copy-done.1 = bf16[8192,128]{1,0:T(8,128)(2,1)S(1)} copy-done((bf16[8192,128]{1,0:T(8,128)(2,1)S(1)}, bf16[8192,128]{1,0:T(8,128)(2,1)}, u32[]{:S(2)}) %copy-start.1) | copy-done | bytes 2097176
  38.0 0.0 copy-start.2
  38.0 29.8 %attend.3 = bf16[8,144,128]{2,1,0:T(8,128)(2,1)S(1)} custom-call(s32[11]{0:T(128)S(1)} %get-tuple-element.5.info, bf16[8,2,128,128]{3,2,1,0:T(8,128)(2,1)S(1)} %bitcast.6, bf16[8192,128]{1,0:T(8,128)(2,1)S(1)} %copy-done.1, bf16[8192,128]{1,0:T(8,128)(2,1)S(1)} %constant_dynamic-update-slice_fusion.2.v_ref), custom_call_target="tpu_custom_call" | custom-call | flops 4294967296 | bytes 6291456 | tf_op jit(solution)/shard_map/attend/pallas_call | solution.py:216
  67.8 1.0 collective-permute-start.2
  68.8 0.0 copy-done.2
  68.8 29.8 %attend.2.a_ref = f32[8,144,128]{2,1,0:T(8,128)S(1)} custom-call(s32[11]{0:T(128)S(1)} %pad_add_fusion.info, bf16[8,2,128,128]{3,2,1,0:T(8,128)(2,1)S(1)} %bitcast.7, bf16[8192,128]{1,0:T(8,128)(2,1)S(1)} %copy-done.2, bf16[8192,128]{1,0:T(8,128)(2,1)S(1)} %constant_dynamic-update-slice_fusion.2.v_ref), custom_call_target="tpu_custom_call" | custom-call | flops 4294967296 | bytes 6291456 | tf_op jit(solution)/shard_map/attend/pallas_call | solution.py:216
  98.6 0.0 collective-permute-done.2.b_ref
  98.6 0.1 merge.1
  98.7 13.7 %all_to_all.10.x_ref = bf16[8,144,128]{2,1,0:T(8,128)(2,1)S(1)} all-to-all(bf16[8,144,128]{2,1,0:T(8,128)(2,1)S(1)} %merge.1), channel_id=1, replica_groups=mesh['z'=8,'y'=2,'c'=2,'h'=2,'x'=4] {'z'}, dimensions={0} | all-to-all | bytes 589824 | tf_op jit(solution)/shard_map/all_to_all | solution.py:288
  112.4 0.8 combine.1
Async XLA Ops:
  0.0 19.0 %collective-permute-start = (bf16[4096,128]{1,0:T(8,128)(2,1)}, bf16[4096,128]{1,0:T(8,128)(2,1)}, u32[]{:S(2)}, u32[]{:S(2)}) collective-permute-start(bf16[4096,128]{1,0:T(8,128)(2,1)} %param.5), channel_id=1, source_target_pairs={{0,8},{8,0},{1,9},{9,1},{2,10},{10,2},{3,11},{11,3},{4,12},{12,4},... | collective-permute-start | bytes 3145736 | tf_op jit(solution)/shard_map/ppermute | solution.py:268
  0.0 21.7 %collective-permute-start.1 = (bf16[4096,128]{1,0:T(8,128)(2,1)}, bf16[4096,128]{1,0:T(8,128)(2,1)}, u32[]{:S(2)}, u32[]{:S(2)}) collective-permute-start(bf16[4096,128]{1,0:T(8,128)(2,1)} %param.6), channel_id=1, source_target_pairs={{0,8},{8,0},{1,9},{9,1},{2,10},{10,2},{3,11},{11,3},{4,12},{12,4},... | collective-permute-start | bytes 3145736 | tf_op jit(solution)/shard_map/ppermute | solution.py:269
  0.5 0.8 copy-start.3
  1.3 17.2 %copy-start.4 = (bf16[4096,128]{1,0:T(8,128)(2,1)S(1)}, bf16[4096,128]{1,0:T(8,128)(2,1)}, u32[]{:S(2)}) copy-start(bf16[4096,128]{1,0:T(8,128)(2,1)} %param.5) | copy-start | bytes 3145732
  2.2 34.2 %all-to-all-start = ((bf16[128,16,128]{2,1,0:T(8,128)(2,1)}), bf16[128,16,128]{2,1,0:T(8,128)(2,1)S(1)}, u32[]{:S(2)}, u32[]{:S(2)}) async-start(bf16[128,16,128]{2,1,0:T(8,128)(2,1)} %bitcast.3), calls=%async_computation | async-start | bytes 1048576 | tf_op jit(solution)/shard_map/all_to_all | solution.py:274
  17.6 1.2 %copy-start.5 = (bf16[4096,128]{1,0:T(8,128)(2,1)S(1)}, bf16[4096,128]{1,0:T(8,128)(2,1)}, u32[]{:S(2)}) copy-start(bf16[4096,128]{1,0:T(8,128)(2,1)} %param.6) | copy-start | bytes 3145732
  20.4 1.3 %copy-start = (bf16[8192,128]{1,0:T(8,128)(2,1)}, bf16[8192,128]{1,0:T(8,128)(2,1)S(1)}, u32[]{:S(2)}) copy-start(bf16[8192,128]{1,0:T(8,128)(2,1)S(1)} %constant_dynamic-update-slice_fusion.k_ref) | copy-start | bytes 6291460
  36.4 1.6 %copy-start.1 = (bf16[8192,128]{1,0:T(8,128)(2,1)S(1)}, bf16[8192,128]{1,0:T(8,128)(2,1)}, u32[]{:S(2)}) copy-start(bf16[8192,128]{1,0:T(8,128)(2,1)} %copy-done) | copy-start | bytes 6291460
  38.0 30.8 %copy-start.2 = (bf16[8192,128]{1,0:T(8,128)(2,1)S(1)}, bf16[8192,128]{1,0:T(8,128)(2,1)}, u32[]{:S(2)}) copy-start(bf16[8192,128]{1,0:T(8,128)(2,1)} %copy-done) | copy-start | bytes 6291460
  67.8 30.8 %collective-permute-start.2 = (bf16[8,144,128]{2,1,0:T(8,128)(2,1)S(1)}, bf16[8,144,128]{2,1,0:T(8,128)(2,1)S(1)}, u32[]{:S(2)}, u32[]{:S(2)}) collective-permute-start(bf16[8,144,128]{2,1,0:T(8,128)(2,1)S(1)} %attend.3), channel_id=1, source_target_pairs={{0,16},{16,0},{1,17},{17,1},{2,18},{18,2},{3,19},{19,3},{4,20},{20... | collective-permute-start | bytes 884744 | tf_op jit(solution)/shard_map/ppermute | solution.py:286

commit v2 on v1

--- a/solution.py
+++ b/solution.py
@@ -12,10 +12,8 @@
 QPK = 8
 CANDS = 8
 HALF = 4096
-LANES = 1024
 CAND_LANES = 128
-MEMBERS = LANES // CAND_LANES
-GROUPS = CANDS // MEMBERS
+LANES = CANDS * CAND_LANES
 SAMPLE = 128
 EXTRA = 16
 NONE = -1e30
@@ -51,111 +49,93 @@
         out_ref[j] = blocks
 
 
-def attend_kernel(info, q_ref, k_ref, v_ref, out_ref, top_ref, acc_ref, sum_ref, big_ref):
+def attend_kernel(info, q_ref, k_ref, v_ref, out_ref, top_ref, acc_ref, sum_ref):
     base_own, base_other, part = info[CANDS], info[CANDS + 1], info[CANDS + 2]
     base = jnp.minimum(base_own, base_other)
     halves = ((0, base_own), (HALF, base_other))
-    lane = lax.broadcasted_iota(jnp.int32, (1, LANES), 1)
-
-    def visible(group):
-        seen = info[group * MEMBERS]
-        for j in range(1, MEMBERS):
-            seen = jnp.where(lane < j * CAND_LANES, seen, info[group * MEMBERS + j])
-        return seen
-
-    def group_queries(group):
-        rows = [q_ref[group * MEMBERS + j, part] for j in range(MEMBERS)]
-        return jnp.concatenate(rows, axis=0)
-
-    def store(group, numerators, total, top):
-        extra = split_total(total, top, LANES)
-        for j in range(MEMBERS):
+    lengths = [info[c] for c in range(CANDS)]
+
+    def per_candidate(values, lane):
+        result = values[0]
+        for c in range(1, CANDS):
+            result = jnp.where(lane < c * CAND_LANES, result, values[c])
+        return result
+
+    def store(first, count, numerators, total, top):
+        extra = split_total(total, top, count * HD)
+        for j in range(count):
             cut = slice(j * HD, (j + 1) * HD)
-            out_ref[group * MEMBERS + j, :HD, :] = numerators[:, cut].astype(out_ref.dtype)
-            out_ref[group * MEMBERS + j, HD:, :] = extra[:, cut].astype(out_ref.dtype)
+            out_ref[first + j, :HD, :] = numerators[:, cut].astype(out_ref.dtype)
+            out_ref[first + j, HD:, :] = extra[:, cut].astype(out_ref.dtype)
+
+    queries = jnp.concatenate([q_ref[c, part] for c in range(CANDS)], axis=0)
 
     first = pl.multiple_of(jnp.where(base_own == base, 0, HALF), HALF)
-    first_keys = k_ref[pl.ds(first, SAMPLE), :]
     place = base + lax.broadcasted_iota(jnp.int32, (SAMPLE, LANES), 0)
-    for group in range(GROUPS):
-        s = scores(first_keys, group_queries(group))
-        top = jnp.max(jnp.where(place < visible(group), s, NONE), axis=0, keepdims=True)
-        top_ref[group] = top.astype(jnp.bfloat16).astype(jnp.float32)
-    big_ref[...] = jnp.zeros_like(big_ref)
-
-    @pl.loop(0, GROUPS)
-    def _(group):
-        lengths = [info[group * MEMBERS + j] for j in range(MEMBERS)]
-        idle = functools.reduce(jnp.maximum, lengths) <= base
-
-        @pl.when(idle)
-        def _():
-            nothing = jnp.zeros((1, LANES), jnp.float32)
-            store(group, jnp.zeros((HD, LANES), jnp.float32), nothing, nothing + NONE)
-
-        @pl.when(jnp.logical_not(idle))
-        def _():
-            column = lax.broadcasted_iota(jnp.int32, (1, HD), 1)
-            limit = functools.reduce(
-                lambda rest, j: jnp.where(column == j, lengths[j], rest),
-                range(MEMBERS),
-                jnp.full((1, HD), 2**30, jnp.int32),
-            )
-            member = lax.broadcasted_iota(jnp.int32, (LANES, HD), 0) // CAND_LANES
-            column = lax.broadcasted_iota(jnp.int32, (LANES, HD), 1)
-            veto = jnp.where(member == column, HIDDEN, 0.0).astype(jnp.bfloat16)
-            query_rows = jnp.concatenate([group_queries(group), veto], axis=1)
-            top = top_ref[group]
-            point = jnp.where(top > 0.5 * NONE, top, -NONE)
-            total = jnp.zeros((8, LANES), jnp.float32)
-            numerators = jnp.zeros((HD, LANES), jnp.float32)
-            for half, start in halves:
-                place = start + lax.broadcasted_iota(jnp.int32, (HALF, HD), 0)
-                unseen = jnp.where(place >= limit, 1.0, 0.0).astype(jnp.bfloat16)
-                key_rows = jnp.concatenate([k_ref[half : half + HALF, :], unseen], axis=1)
-                weights = jnp.exp2(scores(key_rows, query_rows) - point)
-                total += jnp.sum(weights.reshape(HALF // 8, 8, LANES), axis=0)
-                numerators += weighted(v_ref[half : half + HALF, :], weights)
-            total = jnp.sum(total, axis=0, keepdims=True)
-            big_ref[...] = jnp.maximum(big_ref[...], total)
-            store(group, numerators, total, top)
-
-    @pl.when(jnp.logical_not(jnp.max(big_ref[...]) < LIMIT))
+    seen = per_candidate(lengths, lax.broadcasted_iota(jnp.int32, (1, LANES), 1))
+    top = jnp.where(place < seen, scores(k_ref[pl.ds(first, SAMPLE), :], queries), NONE)
+    top = jnp.max(top, axis=0, keepdims=True).astype(jnp.bfloat16).astype(jnp.float32)
+    point = jnp.where(top > 0.5 * NONE, top, -NONE)
+
+    column = lax.broadcasted_iota(jnp.int32, (1, HD), 1)
+    limit = jnp.full((1, HD), 2**30, jnp.int32)
+    for c in range(CANDS):
+        limit = jnp.where(column == c, lengths[c], limit)
+    member = lax.broadcasted_iota(jnp.int32, (LANES, HD), 0) // CAND_LANES
+    column = lax.broadcasted_iota(jnp.int32, (LANES, HD), 1)
+    veto = jnp.where(member == column, HIDDEN, 0.0).astype(jnp.bfloat16)
+    query_rows = jnp.concatenate([queries, veto], axis=1)
+
+    total = jnp.zeros((8, LANES), jnp.float32)
+    numerators = jnp.zeros((HD, LANES), jnp.float32)
+    for half, start in halves:
+        lead = (start + 1 - limit).astype(jnp.float32)
+        row = lax.broadcasted_iota(jnp.int32, (HALF, HD), 0).astype(jnp.float32)
+        beyond = jnp.maximum(row + lead, 0.0).astype(jnp.bfloat16)
+        key_rows = jnp.concatenate([k_ref[half : half + HALF, :], beyond], axis=1)
+        weights = jnp.exp2(scores(key_rows, query_rows) - point)
+        total += jnp.sum(weights.reshape(HALF // 8, 8, LANES), axis=0)
+        numerators += weighted(v_ref[half : half + HALF, :], weights)
+    total = jnp.sum(total, axis=0, keepdims=True)
+    store(0, CANDS, numerators, total, top)
+
+    @pl.when(jnp.logical_not(jnp.max(total) < LIMIT))
     def _():
         block = 512
 
-        @pl.loop(0, GROUPS)
-        def _(group):
-            query_rows = group_queries(group)
-            seen = visible(group)
+        @pl.loop(0, CANDS)
+        def _(c):
+            query_rows = q_ref[c, part]
             acc_ref[...] = jnp.zeros_like(acc_ref)
             sum_ref[...] = jnp.zeros_like(sum_ref)
-            top_ref[group] = jnp.full((1, LANES), NONE, jnp.float32)
+            top_ref[...] = jnp.full_like(top_ref, NONE)
             for half, start in halves:
 
                 @pl.loop(0, HALF // block)
                 def _(i):
                     at = pl.multiple_of(half + i * block, block)
-                    place = start + i * block + lax.broadcasted_iota(jnp.int32, (block, LANES), 0)
-                    usable = place < seen
+                    place = start + i * block + lax.broadcasted_iota(
+                        jnp.int32, (block, CAND_LANES), 0
+                    )
+                    usable = place < info[c]
                     s = jnp.where(usable, scores(k_ref[pl.ds(at, block), :], query_rows), NONE)
-                    old = top_ref[group]
+                    old = top_ref[...]
                     new = jnp.maximum(old, jnp.max(s, axis=0, keepdims=True))
                     shrink = jnp.exp2(old - new)
                     weights = jnp.where(usable, jnp.exp2(s - new), 0.0)
                     sum_ref[...] = sum_ref[...] * shrink + jnp.sum(
-                        weights.reshape(block // 8, 8, LANES), axis=0
+                        weights.reshape(block // 8, 8, CAND_LANES), axis=0
                     )
                     acc_ref[...] = acc_ref[...] * shrink + weighted(
                         v_ref[pl.ds(at, block), :], weights
                     )
-                    top_ref[group] = new
-
-            top = top_ref[group]
+                    top_ref[...] = new
+
+            top = top_ref[...]
             sent = top.astype(jnp.bfloat16).astype(jnp.float32)
             fit = jnp.where(top > 0.5 * NONE, jnp.exp2(top - sent), 1.0)
             total = jnp.sum(sum_ref[...], axis=0, keepdims=True)
-            store(group, acc_ref[...] * fit, total * fit, sent)
+            store(c, 1, acc_ref[...] * fit, total * fit, sent)
 
 
 def split_total(total, top, width):
@@ -219,10 +199,9 @@
         in_specs=[pl.BlockSpec(memory_space=pltpu.SMEM)] + [in_vmem] * 3,
         out_specs=in_vmem,
         scratch_shapes=[
-            pltpu.VMEM((GROUPS, 1, LANES), jnp.float32),
-            pltpu.VMEM((HD, LANES), jnp.float32),
-            pltpu.VMEM((8, LANES), jnp.float32),
-            pltpu.VMEM((1, LANES), jnp.float32),
+            pltpu.VMEM((1, CAND_LANES), jnp.float32),
+            pltpu.VMEM((HD, CAND_LANES), jnp.float32),
+            pltpu.VMEM((8, CAND_LANES), jnp.float32),
         ],
         compiler_params=pltpu.CompilerParams(vmem_limit_bytes=40 * 2**20),
         cost_estimate=pl.CostEstimate(

time: 115 us -> 189 us (1.64)
  Pallas kernels: 61.4 us -> 135 us
    pallas_call x2, Pallas kernels: 59.6 us -> 133 us  [attend(): pl.pallas_call(attend_kernel, out_shape=jax.ShapeDtypeStruct((CANDS, HD +...]
  transfers between devices with their start and end apart: 4 -> 4, of which waited for: 1 -> 1; matrix products, arithmetic and copies ran while one was open for 3% -> 2% of each run, Pallas kernels for 27% -> 36%
where the time goes in v2:
time: 189 us; the launch traced here: 188 us
  Pallas kernels  135 us (71%)
  starting transfers between devices  17.1 us (9%)
  blocking collectives  14.5 us (8%)
  waiting for transfers between devices  13.3 us (7%)
  local copies, waits for them, and re-layouts  6.88 us (4%)
    pallas_call x2, Pallas kernels, attend(): pl.pallas_call(attend_kernel, out_shape=jax.ShapeDtypeStruct((CANDS, HD +...  133 us
    all_to_all x1, starting transfers between devices, body(): lax.all_to_all(blocks.reshape((spans * heads,) + blocks.shape[2:]), ('z',...  15.4 us
    all_to_all x1, blocking collectives, body(): return combine(lax.all_to_all(merge(own, received), 'z', 0, 0))  14.5 us
    all_to_all x1, waiting for transfers between devices, body(): lax.all_to_all(blocks.reshape((spans * heads,) + blocks.shape[2:]), ('z',...  13.3 us
    unnamed x14, local copies, waits for them, and re-layouts  4.15 us
  transfers between devices with their start and end apart: 4, of which 1 were waited for; matrix products, arithmetic and copies ran while one was open for 2% of the time, Pallas kernels for 36%

profile of v2, /device:TPU:2, one launch (start us, length us, event | category | flops | bytes accessed | tf_op | source)
XLA Modules:
  0.0 187.7 jit_solution(14372677310012322793)
XLA Ops:
  0.0 0.0 collective-permute-start
  0.0 0.5 collective-permute-start.1
  0.5 0.0 copy-start.3
  0.5 0.8 copy-done.3
  1.3 0.0 copy-start.4
  1.3 0.9 build_blocks.1
  2.2 15.4 %all-to-all-start = ((bf16[128,16,128]{2,1,0:T(8,128)(2,1)}), bf16[128,16,128]{2,1,0:T(8,128)(2,1)S(1)}, u32[]{:S(2)}, u32[]{:S(2)}) async-start(bf16[128,16,128]{2,1,0:T(8,128)(2,1)} %bitcast.3), calls=%async_computation | async-start | bytes 1048576 | tf_op jit(solution)/shard_map/all_to_all | solution.py:253
  17.6 0.0 copy-start.5
  17.6 0.8 pad_add_fusion.2
  18.5 0.0 copy-done.4
  18.5 0.1 constant_dynamic-update-slice_fusion.1
  18.5 0.3 copy-done.5
  18.9 0.1 constant_dynamic-update-slice_fusion.3
  18.9 0.1 pad_add_fusion.info
  19.0 0.0 collective-permute-done
  19.0 1.4 constant_dynamic-update-slice_fusion.k_ref
  20.4 0.0 copy-start
  20.4 1.3 copy-done
  21.7 0.0 collective-permute-done.1
  21.7 1.4 constant_dynamic-update-slice_fusion.2.v_ref
  23.1 13.3 %all-to-all-done = bf16[128,16,128]{2,1,0:T(8,128)(2,1)S(1)} async-done(((bf16[128,16,128]{2,1,0:T(8,128)(2,1)}), bf16[128,16,128]{2,1,0:T(8,128)(2,1)S(1)}, u32[]{:S(2)}, u32[]{:S(2)}) %all-to-all-start) | async-done | bytes 524320 | tf_op jit(solution)/shard_map/all_to_all | solution.py:253
  36.4 0.0 copy-start.1
  36.4 1.6 copy-done.1
  38.0 0.0 copy-start.2
  38.0 66.6 %attend.3 = bf16[8,144,128]{2,1,0:T(8,128)(2,1)S(1)} custom-call(s32[11]{0:T(128)S(1)} %get-tuple-element.5.info, bf16[8,2,128,128]{3,2,1,0:T(8,128)(2,1)S(1)} %bitcast.6, bf16[8192,128]{1,0:T(8,128)(2,1)S(1)} %copy-done.1, bf16[8192,128]{1,0:T(8,128)(2,1)S(1)} %constant_dynamic-update-slice_fusion.2.v_ref), custom_call_target="tpu_custom_call" | custom-call | flops 4294967296 | bytes 6291456 | tf_op jit(solution)/shard_map/attend/pallas_call | solution.py:196
  104.6 1.2 collective-permute-start.2
  105.8 0.0 copy-done.2
  105.8 66.5 %attend.2.a_ref = f32[8,144,128]{2,1,0:T(8,128)S(1)} custom-call(s32[11]{0:T(128)S(1)} %pad_add_fusion.info, bf16[8,2,128,128]{3,2,1,0:T(8,128)(2,1)S(1)} %bitcast.7, bf16[8192,128]{1,0:T(8,128)(2,1)S(1)} %copy-done.2, bf16[8192,128]{1,0:T(8,128)(2,1)S(1)} %constant_dynamic-update-slice_fusion.2.v_ref), custom_call_target="tpu_custom_call" | custom-call | flops 4294967296 | bytes 6291456 | tf_op jit(solution)/shard_map/attend/pallas_call | solution.py:196
  172.3 0.0 collective-permute-done.2.b_ref
  172.3 0.1 merge.1
  172.4 14.5 %all_to_all.10.x_ref = bf16[8,144,128]{2,1,0:T(8,128)(2,1)S(1)} all-to-all(bf16[8,144,128]{2,1,0:T(8,128)(2,1)S(1)} %merge.1), channel_id=1, replica_groups=mesh['z'=8,'y'=2,'c'=2,'h'=2,'x'=4] {'z'}, dimensions={0} | all-to-all | bytes 589824 | tf_op jit(solution)/shard_map/all_to_all | solution.py:267
  187.0 0.8 combine.1
Async XLA Ops:
  0.0 19.0 %collective-permute-start = (bf16[4096,128]{1,0:T(8,128)(2,1)}, bf16[4096,128]{1,0:T(8,128)(2,1)}, u32[]{:S(2)}, u32[]{:S(2)}) collective-permute-start(bf16[4096,128]{1,0:T(8,128)(2,1)} %param.5), channel_id=1, source_target_pairs={{0,8},{8,0},{1,9},{9,1},{2,10},{10,2},{3,11},{11,3},{4,12},{12,4},... | collective-permute-start | bytes 3145736 | tf_op jit(solution)/shard_map/ppermute | solution.py:247
  0.0 21.7 %collective-permute-start.1 = (bf16[4096,128]{1,0:T(8,128)(2,1)}, bf16[4096,128]{1,0:T(8,128)(2,1)}, u32[]{:S(2)}, u32[]{:S(2)}) collective-permute-start(bf16[4096,128]{1,0:T(8,128)(2,1)} %param.6), channel_id=1, source_target_pairs={{0,8},{8,0},{1,9},{9,1},{2,10},{10,2},{3,11},{11,3},{4,12},{12,4},... | collective-permute-start | bytes 3145736 | tf_op jit(solution)/shard_map/ppermute | solution.py:248
  0.5 0.8 copy-start.3
  1.3 17.2 %copy-start.4 = (bf16[4096,128]{1,0:T(8,128)(2,1)S(1)}, bf16[4096,128]{1,0:T(8,128)(2,1)}, u32[]{:S(2)}) copy-start(bf16[4096,128]{1,0:T(8,128)(2,1)} %param.5) | copy-start | bytes 3145732
  2.2 34.2 %all-to-all-start = ((bf16[128,16,128]{2,1,0:T(8,128)(2,1)}), bf16[128,16,128]{2,1,0:T(8,128)(2,1)S(1)}, u32[]{:S(2)}, u32[]{:S(2)}) async-start(bf16[128,16,128]{2,1,0:T(8,128)(2,1)} %bitcast.3), calls=%async_computation | async-start | bytes 1048576 | tf_op jit(solution)/shard_map/all_to_all | solution.py:253
  17.6 1.2 copy-start.5
  20.4 1.3 copy-start
  36.4 1.6 copy-start.1
  38.0 67.8 %copy-start.2 = (bf16[8192,128]{1,0:T(8,128)(2,1)S(1)}, bf16[8192,128]{1,0:T(8,128)(2,1)}, u32[]{:S(2)}) copy-start(bf16[8192,128]{1,0:T(8,128)(2,1)} %copy-done) | copy-start | bytes 6291460
  104.6 67.7 %collective-permute-start.2 = (bf16[8,144,128]{2,1,0:T(8,128)(2,1)S(1)}, bf16[8,144,128]{2,1,0:T(8,128)(2,1)S(1)}, u32[]{:S(2)}, u32[]{:S(2)}) collective-permute-start(bf16[8,144,128]{2,1,0:T(8,128)(2,1)S(1)} %attend.3), channel_id=1, source_target_pairs={{0,16},{16,0},{1,17},{17,1},{2,18},{18,2},{3,19},{19,3},{4,20},{20... | collective-permute-start | bytes 884744 | tf_op jit(solution)/shard_map/ppermute | solution.py:265

commit v3 on v2

--- a/solution.py
+++ b/solution.py
@@ -50,7 +50,7 @@
 
 
 def attend_kernel(info, q_ref, k_ref, v_ref, out_ref, top_ref, acc_ref, sum_ref):
-    base_own, base_other, part = info[CANDS], info[CANDS + 1], info[CANDS + 2]
+    base_own, base_other = info[CANDS], info[CANDS + 1]
     base = jnp.minimum(base_own, base_other)
     halves = ((0, base_own), (HALF, base_other))
     lengths = [info[c] for c in range(CANDS)]
@@ -68,7 +68,7 @@
             out_ref[first + j, :HD, :] = numerators[:, cut].astype(out_ref.dtype)
             out_ref[first + j, HD:, :] = extra[:, cut].astype(out_ref.dtype)
 
-    queries = jnp.concatenate([q_ref[c, part] for c in range(CANDS)], axis=0)
+    queries = jnp.concatenate([q_ref[c] for c in range(CANDS)], axis=0)
 
     first = pl.multiple_of(jnp.where(base_own == base, 0, HALF), HALF)
     place = base + lax.broadcasted_iota(jnp.int32, (SAMPLE, LANES), 0)
@@ -105,7 +105,7 @@
 
         @pl.loop(0, CANDS)
         def _(c):
-            query_rows = q_ref[c, part]
+            query_rows = q_ref[c]
             acc_ref[...] = jnp.zeros_like(acc_ref)
             sum_ref[...] = jnp.zeros_like(sum_ref)
             top_ref[...] = jnp.full_like(top_ref, NONE)
@@ -192,7 +192,7 @@
 
 def attend(info, q, k, v, dtype):
     in_vmem = pl.BlockSpec(memory_space=pltpu.VMEM)
-    work = q.size // HD // 2 * 2 * HALF
+    work = q.size // HD * 2 * HALF
     return pl.pallas_call(
         attend_kernel,
         out_shape=jax.ShapeDtypeStruct((CANDS, HD + EXTRA, HD), dtype),
@@ -247,23 +247,23 @@
     k = jnp.concatenate([keys, lax.ppermute(keys, "c", swap)], axis=0)
     v = jnp.concatenate([values, lax.ppermute(values, "c", swap)], axis=0)
 
-    heads = lax.axis_size(("h", "x"))
-    spans = lax.axis_size(("z", "y"))
-    blocks = build_blocks(queries, heads, spans)
-    q = lax.all_to_all(
-        blocks.reshape((spans * heads,) + blocks.shape[2:]), ("z", "y", "h", "x"), 0, 0
-    ).reshape(CANDS, spans // CANDS, CAND_LANES, HD)
+    blocks = build_blocks(
+        lax.ppermute(queries, "y", swap), lax.axis_size(("h", "x")), lax.axis_size("z")
+    )
+    q_foreign = lax.all_to_all(
+        blocks.reshape((-1,) + blocks.shape[2:]), ("z", "h", "x"), 0, 0
+    ).reshape(CANDS, CAND_LANES, HD)
+    q_foreign, k, v = lax.optimization_barrier((q_foreign, k, v))
+    q_own = lax.ppermute(q_foreign, "y", swap)
 
     chip = lax.axis_index(("z", "y")) * (2 * HALF)
-    core, side = lax.axis_index("c"), lax.axis_index("y")
-    bases = [chip + core * HALF, chip + (1 - core) * HALF]
-
-    def info(part):
-        return jnp.concatenate([doc_len, jnp.stack(bases + [part]).astype(jnp.int32)])
-
-    foreign = attend(info(1 - side), q, k, v, jnp.bfloat16)
+    core = lax.axis_index("c")
+    bases = jnp.stack([chip + core * HALF, chip + (1 - core) * HALF])
+    info = jnp.concatenate([doc_len, bases.astype(jnp.int32)])
+
+    foreign = attend(info, q_foreign, k, v, jnp.bfloat16)
     received = lax.ppermute(foreign, "y", swap)
-    own = attend(info(side), q, k, v, jnp.float32)
+    own = attend(info, q_own, k, v, jnp.float32)
     return combine(lax.all_to_all(merge(own, received), "z", 0, 0))
 
 

time: 189 us -> 185 us (0.979)
  local copies, waits for them, and re-layouts: 6.88 us -> 1.66 us
  other arithmetic: 0.9 us -> 3.97 us
  waiting for transfers between devices: 13.3 us -> 11.1 us
  starting transfers between devices: 17.1 us -> 19 us
    all_to_all x1, waiting for transfers between devices: 13.3 us -> 9.23 us  [body(): lax.all_to_all(blocks.reshape((-1,) + blocks.shape[2:]), ('z', 'h', 'x'),...]
    concatenate x2 -> x3, other arithmetic: 0.9 us -> 3.97 us  [the longest x1 1.76 us: body(): k = jnp.concatenate([keys, lax.ppermute(keys, 'c', swap)], axis=0)]
    concatenate x2 -> x0, local copies, waits for them, and re-layouts: 2.72 us -> none  [the longest x1 1.36 us: body(): k = jnp.concatenate([keys, lax.ppermute(keys, 'c', swap)], axis=0)]
    unnamed x14 -> x6, local copies, waits for them, and re-layouts: 4.15 us -> 1.66 us
    ppermute x0 -> x2, starting transfers between devices: none -> 2.36 us  [the longest x1 1.58 us: body(): lax.ppermute(queries, 'y', swap)]
  transfers between devices with their start and end apart: 4 -> 6, of which waited for: 1 -> 2; matrix products, arithmetic and copies ran while one was open for 2% -> 2% of each run, Pallas kernels for 36% -> 73%
where the time goes in v3:
time: 185 us; the launch traced here: 184 us
  Pallas kernels  135 us (73%)
  starting transfers between devices  19 us (10%)
  blocking collectives  13.7 us (7%)
  waiting for transfers between devices  11.1 us (6%)
  other arithmetic  3.97 us (2%)
    pallas_call x2, Pallas kernels, attend(): pl.pallas_call(attend_kernel, out_shape=jax.ShapeDtypeStruct((CANDS, HD +...  133 us
    all_to_all x1, starting transfers between devices, body(): lax.all_to_all(blocks.reshape((-1,) + blocks.shape[2:]), ('z', 'h', 'x'),...  14.6 us
    all_to_all x1, blocking collectives, body(): return combine(lax.all_to_all(merge(own, received), 'z', 0, 0))  13.7 us
    all_to_all x1, waiting for transfers between devices, body(): lax.all_to_all(blocks.reshape((-1,) + blocks.shape[2:]), ('z', 'h', 'x'),...  9.23 us
  transfers between devices with their start and end apart: 6, of which 2 were waited for; matrix products, arithmetic and copies ran while one was open for 2% of the time, Pallas kernels for 73%

profile of v3, /device:TPU:2, one launch (start us, length us, event | category | flops | bytes accessed | tf_op | source)
XLA Modules:
  0.0 184.5 jit_solution(13767073472534964726)
XLA Ops:
  0.0 0.0 collective-permute-start.1
  0.0 0.5 collective-permute-start.2
  0.5 1.6 collective-permute-start
  2.1 0.7 pad_add_fusion.info
  2.8 1.8 collective-permute-done.q_ref
  4.6 0.8 build_blocks.1
  5.4 14.6 %all-to-all-start = ((bf16[64,16,128]{2,1,0:T(8,128)(2,1)}), bf16[64,16,128]{2,1,0:T(8,128)(2,1)S(1)}, u32[]{:S(2)}, u32[]{:S(2)}) async-start(bf16[64,16,128]{2,1,0:T(8,128)(2,1)} %bitcast.2), calls=%async_computation | async-start | bytes 524288 | tf_op jit(solution)/shard_map/all_to_all | solution.py:253
  20.1 0.0 copy-start.2
  20.1 0.0 collective-permute-done.1
  20.1 1.8 pad_maximum_fusion.k_ref
  21.8 0.0 collective-permute-done.2
  21.9 0.1 copy-done.2
  21.9 1.5 pad_maximum_fusion.1.v_ref
  23.4 9.2 %all-to-all-done = bf16[64,16,128]{2,1,0:T(8,128)(2,1)S(1)} async-done(((bf16[64,16,128]{2,1,0:T(8,128)(2,1)}), bf16[64,16,128]{2,1,0:T(8,128)(2,1)S(1)}, u32[]{:S(2)}, u32[]{:S(2)}) %all-to-all-start) | async-done | bytes 262176 | tf_op jit(solution)/shard_map/all_to_all | solution.py:253
  32.6 0.8 collective-permute-start.3
  33.4 0.0 copy-start
  33.4 1.6 copy-done
  35.0 0.0 copy-start.1
  35.0 66.7 %attend.3 = bf16[8,144,128]{2,1,0:T(8,128)(2,1)S(1)} custom-call(s32[10]{0:T(128)S(1)} %pad_add_fusion.info, bf16[8,128,128]{2,1,0:T(8,128)(2,1)S(1)} %bitcast.5, bf16[8192,128]{1,0:T(8,128)(2,1)S(1)} %pad_maximum_fusion.k_ref, bf16[8192,128]{1,0:T(8,128)(2,1)S(1)} %copy-done), custom_call_target="tpu_custom_call" | custom-call | flops 4294967296 | bytes 6291456 | tf_op jit(solution)/shard_map/attend/pallas_call | solution.py:196
  101.7 1.5 collective-permute-start.4
  103.2 0.0 collective-permute-done.3.q_ref
  103.2 0.0 copy-done.1
  103.2 66.6 %attend.2.a_ref = f32[8,144,128]{2,1,0:T(8,128)S(1)} custom-call(s32[10]{0:T(128)S(1)} %pad_add_fusion.info, bf16[8,128,128]{2,1,0:T(8,128)(2,1)S(1)} %collective-permute-done.3.q_ref, bf16[8192,128]{1,0:T(8,128)(2,1)S(1)} %pad_maximum_fusion.k_ref, bf16[8192,128]{1,0:T(8,128)(2,1)S(1)} %copy-done.1), custom_call_target="tpu_custom_call" | custom-call | flops 4294967296 | bytes 6291456 | tf_op jit(solution)/shard_map/attend/pallas_call | solution.py:196
  169.8 0.0 collective-permute-done.4.b_ref
  169.9 0.1 merge.1
  170.0 13.7 %all_to_all.10.x_ref = bf16[8,144,128]{2,1,0:T(8,128)(2,1)S(1)} all-to-all(bf16[8,144,128]{2,1,0:T(8,128)(2,1)S(1)} %merge.1), channel_id=1, replica_groups=mesh['z'=8,'y'=2,'c'=2,'h'=2,'x'=4] {'z'}, dimensions={0} | all-to-all | bytes 589824 | tf_op jit(solution)/shard_map/all_to_all | solution.py:267
  183.7 0.8 combine.1
Async XLA Ops:
  0.0 20.1 %collective-permute-start.1 = (bf16[4096,128]{1,0:T(8,128)(2,1)}, bf16[4096,128]{1,0:T(8,128)(2,1)}, u32[]{:S(2)}, u32[]{:S(2)}) collective-permute-start(bf16[4096,128]{1,0:T(8,128)(2,1)} %param.5), channel_id=1, source_target_pairs={{0,8},{8,0},{1,9},{9,1},{2,10},{10,2},{3,11},{11,3},{4,12},{12,4},... | collective-permute-start | bytes 3145736 | tf_op jit(solution)/shard_map/ppermute | solution.py:247
  0.0 21.8 %collective-permute-start.2 = (bf16[4096,128]{1,0:T(8,128)(2,1)}, bf16[4096,128]{1,0:T(8,128)(2,1)S(1)}, u32[]{:S(2)}, u32[]{:S(2)}) collective-permute-start(bf16[4096,128]{1,0:T(8,128)(2,1)} %param.6), channel_id=1, source_target_pairs={{0,8},{8,0},{1,9},{9,1},{2,10},{10,2},{3,11},{11,3},{4,12},{12,4},... | collective-permute-start | bytes 3145736 | tf_op jit(solution)/shard_map/ppermute | solution.py:248
  0.5 4.1 %collective-permute-start = (bf16[2,8192]{1,0:T(2,128)(2,1)}, bf16[2,8192]{1,0:T(2,128)(2,1)S(1)}, u32[]{:S(2)}, u32[]{:S(2)}) collective-permute-start(bf16[2,8192]{1,0:T(2,128)(2,1)} %param.4), channel_id=1, source_target_pairs={{0,16},{16,0},{1,17},{17,1},{2,18},{18,2},{3,19},{19,3},{4,20},{20... | collective-permute-start | bytes 98312 | tf_op jit(solution)/shard_map/ppermute | solution.py:251
  5.4 27.2 %all-to-all-start = ((bf16[64,16,128]{2,1,0:T(8,128)(2,1)}), bf16[64,16,128]{2,1,0:T(8,128)(2,1)S(1)}, u32[]{:S(2)}, u32[]{:S(2)}) async-start(bf16[64,16,128]{2,1,0:T(8,128)(2,1)} %bitcast.2), calls=%async_computation | async-start | bytes 524288 | tf_op jit(solution)/shard_map/all_to_all | solution.py:253
  20.1 1.9 %copy-start.2 = (bf16[4096,128]{1,0:T(8,128)(2,1)S(1)}, bf16[4096,128]{1,0:T(8,128)(2,1)}, u32[]{:S(2)}) copy-start(bf16[4096,128]{1,0:T(8,128)(2,1)} %param.6) | copy-start | bytes 3145732
  32.6 70.6 %collective-permute-start.3 = (bf16[8,128,128]{2,1,0:T(8,128)(2,1)S(1)}, bf16[8,128,128]{2,1,0:T(8,128)(2,1)S(1)}, u32[]{:S(2)}, u32[]{:S(2)}) collective-permute-start(bf16[8,128,128]{2,1,0:T(8,128)(2,1)S(1)} %bitcast.4), channel_id=1, source_target_pairs={{0,16},{16,0},{1,17},{17,1},{2,18},{18,2},{3,19},{19,3},{4,20},{20... | collective-permute-start | bytes 786440 | tf_op jit(solution)/shard_map/ppermute | solution.py:257
  33.4 1.6 copy-start
  35.0 68.2 %copy-start.1 = (bf16[8192,128]{1,0:T(8,128)(2,1)S(1)}, bf16[8192,128]{1,0:T(8,128)(2,1)}, u32[]{:S(2)}) copy-start(bf16[8192,128]{1,0:T(8,128)(2,1)} %pad_maximum_fusion.1.v_ref) | copy-start | bytes 6291460
  101.7 68.2 %collective-permute-start.4 = (bf16[8,144,128]{2,1,0:T(8,128)(2,1)S(1)}, bf16[8,144,128]{2,1,0:T(8,128)(2,1)S(1)}, u32[]{:S(2)}, u32[]{:S(2)}) collective-permute-start(bf16[8,144,128]{2,1,0:T(8,128)(2,1)S(1)} %attend.3), channel_id=1, source_target_pairs={{0,16},{16,0},{1,17},{17,1},{2,18},{18,2},{3,19},{19,3},{4,20},{20... | collective-permute-start | bytes 884744 | tf_op jit(solution)/shard_map/ppermute | solution.py:265

commit v4 on v3

--- a/solution.py
+++ b/solution.py
@@ -49,7 +49,21 @@
         out_ref[j] = blocks
 
 
-def attend_kernel(info, q_ref, k_ref, v_ref, out_ref, top_ref, acc_ref, sum_ref):
+def fetching_kernel(
+    info, q_ref, k_ref, v_own, v_other, out_ref, top_ref, acc_ref, sum_ref, v_ref, arrived
+):
+    copies = [
+        pltpu.make_async_copy(v_own, v_ref.at[:HALF], arrived.at[0]),
+        pltpu.make_async_copy(v_other, v_ref.at[HALF:], arrived.at[1]),
+    ]
+    for copy in copies:
+        copy.start()
+    attend_kernel(info, q_ref, k_ref, v_ref, out_ref, top_ref, acc_ref, sum_ref, copies)
+
+
+def attend_kernel(
+    info, q_ref, k_ref, v_ref, out_ref, top_ref, acc_ref, sum_ref, copies=(None, None)
+):
     base_own, base_other = info[CANDS], info[CANDS + 1]
     base = jnp.minimum(base_own, base_other)
     halves = ((0, base_own), (HALF, base_other))
@@ -88,7 +102,9 @@
 
     total = jnp.zeros((8, LANES), jnp.float32)
     numerators = jnp.zeros((HD, LANES), jnp.float32)
-    for half, start in halves:
+    for copy, (half, start) in zip(copies, halves, strict=True):
+        if copy is not None:
+            copy.wait()
         lead = (start + 1 - limit).astype(jnp.float32)
         row = lax.broadcasted_iota(jnp.int32, (HALF, HD), 0).astype(jnp.float32)
         beyond = jnp.maximum(row + lead, 0.0).astype(jnp.bfloat16)
@@ -190,25 +206,34 @@
     )(queries)
 
 
-def attend(info, q, k, v, dtype):
+def attend(info, q, k, values, dtype):
     in_vmem = pl.BlockSpec(memory_space=pltpu.VMEM)
     work = q.size // HD * 2 * HALF
+    kernel, value_specs, extra_scratch = attend_kernel, [in_vmem], []
+    if len(values) == 2:
+        kernel = fetching_kernel
+        value_specs = [pl.BlockSpec(memory_space=pltpu.HBM)] * 2
+        extra_scratch = [
+            pltpu.VMEM((2 * HALF, HD), jnp.bfloat16),
+            pltpu.SemaphoreType.DMA((2,)),
+        ]
     return pl.pallas_call(
-        attend_kernel,
+        kernel,
         out_shape=jax.ShapeDtypeStruct((CANDS, HD + EXTRA, HD), dtype),
-        in_specs=[pl.BlockSpec(memory_space=pltpu.SMEM)] + [in_vmem] * 3,
+        in_specs=[pl.BlockSpec(memory_space=pltpu.SMEM)] + [in_vmem] * 2 + value_specs,
         out_specs=in_vmem,
         scratch_shapes=[
             pltpu.VMEM((1, CAND_LANES), jnp.float32),
             pltpu.VMEM((HD, CAND_LANES), jnp.float32),
             pltpu.VMEM((8, CAND_LANES), jnp.float32),
-        ],
+        ]
+        + extra_scratch,
         compiler_params=pltpu.CompilerParams(vmem_limit_bytes=40 * 2**20),
         cost_estimate=pl.CostEstimate(
             flops=4 * work * HD, bytes_accessed=6 * 2**20, transcendentals=work
         ),
         name="attend",
-    )(info, q, k, v)
+    )(info, q, k, *values)
 
 
 def merge(a, b):
@@ -245,7 +270,8 @@
 def body(queries, keys, values, doc_len):
     swap = [(0, 1), (1, 0)]
     k = jnp.concatenate([keys, lax.ppermute(keys, "c", swap)], axis=0)
-    v = jnp.concatenate([values, lax.ppermute(values, "c", swap)], axis=0)
+    v_other = lax.ppermute(values, "c", swap)
+    v = jnp.concatenate([values, v_other], axis=0)
 
     blocks = build_blocks(
         lax.ppermute(queries, "y", swap), lax.axis_size(("h", "x")), lax.axis_size("z")
@@ -261,9 +287,9 @@
     bases = jnp.stack([chip + core * HALF, chip + (1 - core) * HALF])
     info = jnp.concatenate([doc_len, bases.astype(jnp.int32)])
 
-    foreign = attend(info, q_foreign, k, v, jnp.bfloat16)
+    foreign = attend(info, q_foreign, k, (values, v_other), jnp.bfloat16)
     received = lax.ppermute(foreign, "y", swap)
-    own = attend(info, q_own, k, v, jnp.float32)
+    own = attend(info, q_own, k, (v,), jnp.float32)
     return combine(lax.all_to_all(merge(own, received), "z", 0, 0))
 
 

time: 185 us -> 184 us (level)
  transfers between devices with their start and end apart: 6 -> 6, of which waited for: 2 -> 2; matrix products, arithmetic and copies ran while one was open for 2% -> 3% of each run, Pallas kernels for 73% -> 73%
where the time goes in v4:
time: 184 us
  Pallas kernels  136 us (74%)
  starting transfers between devices  18.6 us (10%)
  blocking collectives  14.3 us (8%)
  waiting for transfers between devices  9.65 us (5%)
  other arithmetic  5.2 us (3%)
    pallas_call x2, Pallas kernels, attend(): pl.pallas_call(kernel, out_shape=jax.ShapeDtypeStruct((CANDS, HD + EXTRA,...  134 us
    all_to_all x1, starting transfers between devices, body(): lax.all_to_all(blocks.reshape((-1,) + blocks.shape[2:]), ('z', 'h', 'x'),...  14.6 us
    all_to_all x1, blocking collectives, body(): return combine(lax.all_to_all(merge(own, received), 'z', 0, 0))  14.3 us
    all_to_all x1, waiting for transfers between devices, body(): lax.all_to_all(blocks.reshape((-1,) + blocks.shape[2:]), ('z', 'h', 'x'),...  8.05 us
  transfers between devices with their start and end apart: 6, of which 2 were waited for; matrix products, arithmetic and copies ran while one was open for 3% of the time, Pallas kernels for 73%

profile of v4, /device:TPU:2, one launch (start us, length us, event | category | flops | bytes accessed | tf_op | source)
XLA Modules:
  0.0 183.9 jit_solution(8434043213422078885)
XLA Ops:
  0.0 0.0 collective-permute-start.1
  0.0 1.6 collective-permute-start
  1.6 0.2 collective-permute-start.2
  1.8 0.7 pad_add_fusion.info
  2.5 1.6 collective-permute-done.q_ref
  4.1 0.8 build_blocks.1
  4.9 14.6 %all-to-all-start = ((bf16[64,16,128]{2,1,0:T(8,128)(2,1)}), bf16[64,16,128]{2,1,0:T(8,128)(2,1)S(1)}, u32[]{:S(2)}, u32[]{:S(2)}) async-start(bf16[64,16,128]{2,1,0:T(8,128)(2,1)} %bitcast.2), calls=%async_computation | async-start | bytes 524288 | tf_op jit(solution)/shard_map/all_to_all | solution.py:279
  19.6 0.0 copy-start.1
  19.6 0.0 collective-permute-done.1
  19.6 1.8 pad_maximum_fusion.k_ref
  21.3 0.0 collective-permute-done.2.v_other
  21.4 0.1 copy-done.1
  21.4 2.7 %pad_maximum_fusion.1.v_ref = bf16[8192,128]{1,0:T(8,128)(2,1)} fusion(bf16[4096,128]{1,0:T(8,128)(2,1)} %collective-permute-done.2.v_other, bf16[4096,128]{1,0:T(8,128)(2,1)S(1)} %copy-done.1), kind=kLoop, calls=%fused_computation.1 | loop fusion | flops 4194304 | bytes 4194304 | tf_op jit(solution)/shard_map/concatenate | solution.py:274
  24.1 8.0 %all-to-all-done = bf16[64,16,128]{2,1,0:T(8,128)(2,1)S(1)} async-done(((bf16[64,16,128]{2,1,0:T(8,128)(2,1)}), bf16[64,16,128]{2,1,0:T(8,128)(2,1)S(1)}, u32[]{:S(2)}, u32[]{:S(2)}) %all-to-all-start) | async-done | bytes 262176 | tf_op jit(solution)/shard_map/all_to_all | solution.py:279
  32.2 0.0 copy-start
  32.2 0.7 collective-permute-start.3
  32.8 67.6 %attend.3 = bf16[8,144,128]{2,1,0:T(8,128)(2,1)S(1)} custom-call(s32[10]{0:T(128)S(1)} %pad_add_fusion.info, bf16[8,128,128]{2,1,0:T(8,128)(2,1)S(1)} %bitcast.5, bf16[8192,128]{1,0:T(8,128)(2,1)S(1)} %pad_maximum_fusion.k_ref, bf16[4096,128]{1,0:T(8,128)(2,1)S(1)} %copy-done.1, bf16[4096,128]{1,0:T(8,128)(2,1)} %collective-permute-done.2.v_other), custom_call_target="tpu_custom_call" | custom-call | flops 4294967296 | bytes 6291456 | tf_op jit(solution)/shard_map/attend/pallas_call | solution.py:220
  100.5 1.4 collective-permute-start.4
  101.9 0.0 collective-permute-done.3.q_ref
  101.9 0.0 copy-done
  101.9 66.8 %attend.2.a_ref = f32[8,144,128]{2,1,0:T(8,128)S(1)} custom-call(s32[10]{0:T(128)S(1)} %pad_add_fusion.info, bf16[8,128,128]{2,1,0:T(8,128)(2,1)S(1)} %collective-permute-done.3.q_ref, bf16[8192,128]{1,0:T(8,128)(2,1)S(1)} %pad_maximum_fusion.k_ref, bf16[8192,128]{1,0:T(8,128)(2,1)S(1)} %copy-done), custom_call_target="tpu_custom_call" | custom-call | flops 4294967296 | bytes 6291456 | tf_op jit(solution)/shard_map/attend/pallas_call | solution.py:220
  168.7 0.0 collective-permute-done.4.b_ref
  168.7 0.1 merge.1
  168.8 14.3 %all_to_all.10.x_ref = bf16[8,144,128]{2,1,0:T(8,128)(2,1)S(1)} all-to-all(bf16[8,144,128]{2,1,0:T(8,128)(2,1)S(1)} %merge.1), channel_id=1, replica_groups=mesh['z'=8,'y'=2,'c'=2,'h'=2,'x'=4] {'z'}, dimensions={0} | all-to-all | bytes 589824 | tf_op jit(solution)/shard_map/all_to_all | solution.py:293
  183.2 0.8 combine.1
Async XLA Ops:
  0.0 19.6 %collective-permute-start.1 = (bf16[4096,128]{1,0:T(8,128)(2,1)}, bf16[4096,128]{1,0:T(8,128)(2,1)}, u32[]{:S(2)}, u32[]{:S(2)}) collective-permute-start(bf16[4096,128]{1,0:T(8,128)(2,1)} %param.5), channel_id=1, source_target_pairs={{0,8},{8,0},{1,9},{9,1},{2,10},{10,2},{3,11},{11,3},{4,12},{12,4},... | collective-permute-start | bytes 3145736 | tf_op jit(solution)/shard_map/ppermute | solution.py:272
  0.0 4.1 %collective-permute-start = (bf16[2,8192]{1,0:T(2,128)(2,1)}, bf16[2,8192]{1,0:T(2,128)(2,1)S(1)}, u32[]{:S(2)}, u32[]{:S(2)}) collective-permute-start(bf16[2,8192]{1,0:T(2,128)(2,1)} %param.4), channel_id=1, source_target_pairs={{0,16},{16,0},{1,17},{17,1},{2,18},{18,2},{3,19},{19,3},{4,20},{20... | collective-permute-start | bytes 98312 | tf_op jit(solution)/shard_map/ppermute | solution.py:277
  1.6 19.8 %collective-permute-start.2 = (bf16[4096,128]{1,0:T(8,128)(2,1)}, bf16[4096,128]{1,0:T(8,128)(2,1)}, u32[]{:S(2)}, u32[]{:S(2)}) collective-permute-start(bf16[4096,128]{1,0:T(8,128)(2,1)} %v_own.1), channel_id=1, source_target_pairs={{0,8},{8,0},{1,9},{9,1},{2,10},{10,2},{3,11},{11,3},{4,12},{12,4},... | collective-permute-start | bytes 3145736 | tf_op jit(solution)/shard_map/ppermute | solution.py:273
  4.9 27.3 %all-to-all-start = ((bf16[64,16,128]{2,1,0:T(8,128)(2,1)}), bf16[64,16,128]{2,1,0:T(8,128)(2,1)S(1)}, u32[]{:S(2)}, u32[]{:S(2)}) async-start(bf16[64,16,128]{2,1,0:T(8,128)(2,1)} %bitcast.2), calls=%async_computation | async-start | bytes 524288 | tf_op jit(solution)/shard_map/all_to_all | solution.py:279
  19.6 1.9 %copy-start.1 = (bf16[4096,128]{1,0:T(8,128)(2,1)S(1)}, bf16[4096,128]{1,0:T(8,128)(2,1)}, u32[]{:S(2)}) copy-start(bf16[4096,128]{1,0:T(8,128)(2,1)} %v_own.1) | copy-start | bytes 3145732
  32.2 69.8 %copy-start = (bf16[8192,128]{1,0:T(8,128)(2,1)S(1)}, bf16[8192,128]{1,0:T(8,128)(2,1)}, u32[]{:S(2)}) copy-start(bf16[8192,128]{1,0:T(8,128)(2,1)} %pad_maximum_fusion.1.v_ref) | copy-start | bytes 6291460
  32.2 69.7 %collective-permute-start.3 = (bf16[8,128,128]{2,1,0:T(8,128)(2,1)S(1)}, bf16[8,128,128]{2,1,0:T(8,128)(2,1)S(1)}, u32[]{:S(2)}, u32[]{:S(2)}) collective-permute-start(bf16[8,128,128]{2,1,0:T(8,128)(2,1)S(1)} %bitcast.4), channel_id=1, source_target_pairs={{0,16},{16,0},{1,17},{17,1},{2,18},{18,2},{3,19},{19,3},{4,20},{20... | collective-permute-start | bytes 786440 | tf_op jit(solution)/shard_map/ppermute | solution.py:283
  100.5 68.2 %collective-permute-start.4 = (bf16[8,144,128]{2,1,0:T(8,128)(2,1)S(1)}, bf16[8,144,128]{2,1,0:T(8,128)(2,1)S(1)}, u32[]{:S(2)}, u32[]{:S(2)}) collective-permute-start(bf16[8,144,128]{2,1,0:T(8,128)(2,1)S(1)} %attend.3), channel_id=1, source_target_pairs={{0,16},{16,0},{1,17},{17,1},{2,18},{18,2},{3,19},{19,3},{4,20},{20... | collective-permute-start | bytes 884744 | tf_op jit(solution)/shard_map/ppermute | solution.py:291
